TPU v7x, 32 devices: a whole 2x2x4 slice. The times are simulated.
32 devices in a mesh: gx: 8 (over y, x, core), gy: 4 (over z).
Axes of the slice: x: 2, y: 2, z: 4, core: 2. Of those that a mesh axis runs over, the one named last changes fastest.
Arguments:
- concentration: bfloat16 [128, 128, 512], P(None, 'gx', 'gy'), may hold values from 0.099609375 to 1
- adjoint_next: bfloat16 [128, 128, 512], P(None, 'gx', 'gy'), may hold values from 0 to 2
- sign_x: int32 [128, 512], P('gx', 'gy'), may hold values from 0 to 1
- sign_y: int32 [128, 512], P('gx', 'gy'), may hold values from 0 to 1
- courant_x: float32 [128, 512], P('gx', 'gy'), may hold values from 0.05 to 0.24
- courant_y: float32 [128, 512], P('gx', 'gy'), may hold values from 0.05 to 0.24
- active: int32 [128, 512], P('gx', 'gy'), may hold values from 0 to 1, as said below
- kernel_a: float32 [128], replicated, may hold values from 0.01 to 0.1
- kernel_b: float32 [128], replicated, may hold values from 0.01 to 0.1
Outputs:
- gradient: float32 [128, 128, 512], P(None, 'gx', 'gy')
Inputs may be any that keep to these rules, and one draw needn't show every extreme that they name: Among the devices that share one gy index, 2 hold exactly 2048 active cells (all of their cells) and the others exactly 256; which devices hold more is drawn anew.
All inputs are finite; a program needn't handle non-finite values.
Results may differ from a plain program's by a relative error of at most 0.0003.
Values sent between devices are 32-bit elements; how exact they have to be, the bound alone decides.
A program may use at most 64 MiB of HBM per device.

v0:
```python
import functools

import jax
import jax.numpy as jnp
import numpy as np
from jax import lax
from jax.experimental import pallas as pl
from jax.experimental.pallas import tpu as pltpu
from jax.sharding import PartitionSpec as P

SUBSTEPS = 4
F32 = jnp.float32
BF16 = jnp.bfloat16


def dft_tables(bins):
    freq = 2 * np.arange(bins) + 1
    index = np.arange(bins)
    angle = np.pi * (freq[:, None] * index[None, :] % (4 * bins)) / (2 * bins)
    forward = np.concatenate([np.cos(angle), -np.sin(angle)], axis=0)

    def inverse(outputs):
        phase = np.pi * (outputs[:, None] * freq[None, :] % (4 * bins)) / (2 * bins)
        return np.concatenate([np.cos(phase), -np.sin(phase)], axis=1) / bins

    gain = inverse(index - 1) * (index > 0)[:, None]
    lag = inverse(index + 1)
    return tuple(np.asarray(t, np.float32) for t in (forward, gain, lag))


def split(values):
    high = values.astype(BF16)
    low = (values - high.astype(F32)).astype(BF16)
    return high, low


def stacked(values):
    high, low = split(values)
    return jnp.concatenate([high, low, high], axis=0)


def table3(values):
    high, low = split(values)
    return jnp.concatenate([high, high, low], axis=1)


def dot(table, values):
    return jnp.dot(table, values, preferred_element_type=F32)


def product(left, right):
    half = left.shape[0] // 2
    lr, li, rr, ri = left[:half], left[half:], right[:half], right[half:]
    return jnp.concatenate([lr * rr - li * ri, lr * ri + li * rr], axis=0)


def product_conj(left, right):
    half = left.shape[0] // 2
    lr, li, rr, ri = left[:half], left[half:], right[:half], right[half:]
    return jnp.concatenate([lr * rr + li * ri, li * rr - lr * ri], axis=0)


def kernel(
    n_gx, n_gy, width_x,
    conc, adj, sx, sy, cx, cy, active, ka_ref, kb_ref, fwd_ref, gain_ref, lag_ref,
    out,
    wide, wide_adj, state, lam, y_send, y_recv, z_send, z_recv, moved, faces, t_fwd, t_gain, t_lam, t_lag,
    send_sem, recv_sem,
):
    bins = ka_ref.shape[1]
    width_y = sx.shape[1]
    gx = lax.axis_index("gx")
    gy = lax.axis_index("gy")
    nxt_x, prv_x = lax.rem(gx + 1, n_gx), lax.rem(gx + n_gx - 1, n_gx)
    nxt_y, prv_y = jnp.minimum(gy + 1, n_gy - 1), jnp.maximum(gy - 1, 0)
    has_prv, has_nxt = gy > 0, gy < n_gy - 1
    mesh_id = pl.DeviceIdType.MESH

    barrier = pltpu.get_barrier_semaphore()
    pl.semaphore_signal(barrier, inc=1, device_id=(prv_x, gy), device_id_type=mesh_id)
    pl.semaphore_signal(barrier, inc=1, device_id=(nxt_x, gy), device_id_type=mesh_id)

    @pl.when(has_prv)
    def _():
        pl.semaphore_signal(barrier, inc=1, device_id=(gx, prv_y), device_id_type=mesh_id)

    @pl.when(has_nxt)
    def _():
        pl.semaphore_signal(barrier, inc=1, device_id=(gx, nxt_y), device_id_type=mesh_id)

    lane = lax.broadcasted_iota(jnp.int32, (bins, width_y), 1)
    lane_x = lax.broadcasted_iota(jnp.int32, (width_x, width_y), 1)

    plus_x = sx[...].astype(F32)
    plus_y = sy[...].astype(F32)
    inside = (lane_x + gy * width_y > 0).astype(F32)
    ux = cx[...] * plus_x
    bx = cx[...] * (1.0 - plus_x)
    uy = cy[...] * plus_y * inside
    by = cy[...] * (1.0 - plus_y) * inside

    wide[...] = conc[...].astype(F32)
    for x in range(width_x):
        state[x + 1, :bins, :] = wide[pl.ds(x, bins, stride=width_x), :]
    state[1, bins:bins + 1, :] = ux[0:1]
    state[1, bins + 1:bins + 2, :] = bx[0:1]
    state[1, bins + 2:, :] = jnp.zeros((6, width_y), F32)
    state[width_x, bins:, :] = jnp.zeros((8, width_y), F32)

    def edges(field, buffer):
        to_prv = jnp.zeros((bins, width_y), F32)
        to_nxt = jnp.zeros((bins, width_y), F32)
        for x in range(width_x):
            slab = field[x + 1, :bins, :]
            at_low = pltpu.roll(slab, x, 1) if x else slab
            to_prv = jnp.where(lane == x, at_low, to_prv)
            to_nxt = jnp.where(lane == x, pltpu.roll(slab, x + 1, 1), to_nxt)
        buffer[0, :bins, :] = to_prv
        buffer[1, :bins, :] = to_nxt

    edges(state, y_send)
    y_send[0, bins:bins + width_x, :] = uy
    y_send[0, bins + width_x:, :] = by
    y_send[1, bins:, :] = jnp.zeros((2 * width_x, width_y), F32)

    def x_copies(field, base):
        return (
            pltpu.make_async_remote_copy(
                src_ref=field.at[1], dst_ref=field.at[width_x + 1],
                send_sem=send_sem.at[base], recv_sem=recv_sem.at[base],
                device_id=(prv_x, gy), device_id_type=mesh_id),
            pltpu.make_async_remote_copy(
                src_ref=field.at[width_x], dst_ref=field.at[0],
                send_sem=send_sem.at[base + 1], recv_sem=recv_sem.at[base + 1],
                device_id=(nxt_x, gy), device_id_type=mesh_id),
        )

    def y_copies(source, target, base):
        return (
            pltpu.make_async_remote_copy(
                src_ref=source.at[0], dst_ref=target.at[1],
                send_sem=send_sem.at[base], recv_sem=recv_sem.at[base],
                device_id=(gx, prv_y), device_id_type=mesh_id),
            pltpu.make_async_remote_copy(
                src_ref=source.at[1], dst_ref=target.at[0],
                send_sem=send_sem.at[base + 1], recv_sem=recv_sem.at[base + 1],
                device_id=(gx, nxt_y), device_id_type=mesh_id),
        )

    def start_y(copies, target):
        to_prv, to_nxt = copies

        @pl.when(has_prv)
        def _():
            to_prv.start()

        @pl.when(has_nxt)
        def _():
            to_nxt.start()

        @pl.when(jnp.logical_not(has_prv))
        def _():
            target[0] = jnp.zeros(target.shape[1:], F32)

        @pl.when(jnp.logical_not(has_nxt))
        def _():
            target[1] = jnp.zeros(target.shape[1:], F32)

    def wait_y(copies):
        to_prv, to_nxt = copies

        @pl.when(has_prv)
        def _():
            to_prv.wait_send()
            to_nxt.wait_recv()

        @pl.when(has_nxt)
        def _():
            to_nxt.wait_send()
            to_prv.wait_recv()

    pl.semaphore_wait(barrier, 2 + has_prv.astype(jnp.int32) + has_nxt.astype(jnp.int32))
    first_x = x_copies(state, 0)
    first_y = y_copies(y_send, y_recv, 2)
    start_y(first_y, y_recv)
    for copy in first_x:
        copy.start()

    ka_row, kb_row = ka_ref[...], kb_ref[...]
    ka_full = jnp.broadcast_to(ka_row, (bins, bins))
    kb_full = jnp.broadcast_to(kb_row, (bins, bins))
    ka_col, kb_col = ka_full.T, kb_full.T
    pair = ka_col * kb_full + kb_col * ka_full
    forward = fwd_ref[...]
    t_fwd[0:2 * bins, :] = table3(forward * ka_row)
    t_fwd[2 * bins:4 * bins, :] = table3(forward * kb_row)
    t_fwd[4 * bins:, :] = table3(pair)
    t_gain[...] = table3(gain_ref[...])
    t_lam[...] = table3(forward)
    lag = lag_ref[...]
    ka_col2 = jnp.concatenate([ka_col, ka_col], axis=1)
    kb_col2 = jnp.concatenate([kb_col, kb_col], axis=1)
    t_lag[:, :6 * bins] = table3(ka_col2 * lag)
    t_lag[:, 6 * bins:12 * bins] = table3(kb_col2 * lag)
    t_lag[:, 12 * bins:] = table3(-pair)

    wide_adj[...] = adj[...].astype(F32)

    wait_y(first_y)
    for copy in first_x:
        copy.wait()

    ux_next = jnp.concatenate([ux[1:], state[width_x + 1, bins:bins + 1, :]], axis=0)
    bx_next = jnp.concatenate([bx[1:], state[width_x + 1, bins + 1:bins + 2, :]], axis=0)
    last_lane = lane_x == width_y - 1
    uy_next = jnp.where(
        last_lane, pltpu.roll(y_recv[1, bins:bins + width_x, :], width_y - 1, 1), pltpu.roll(uy, width_y - 1, 1))
    by_next = jnp.where(
        last_lane, pltpu.roll(y_recv[1, bins + width_x:, :], width_y - 1, 1), pltpu.roll(by, width_y - 1, 1))
    centre = 1.0 - bx - ux_next - by - uy_next
    for index, values in enumerate((centre, ux, bx, ux_next, bx_next, uy, by, uy_next, by_next)):
        faces[index] = values

    def stencil(field, halo, x, low_x, high_x, low_y, high_y):
        slab = field[x + 1, :bins, :]
        before = jnp.where(lane == 0, pltpu.roll(halo[0, :bins, :], (width_y - x) % width_y, 1), pltpu.roll(slab, 1, 1))
        after = jnp.where(
            lane == width_y - 1, pltpu.roll(halo[1, :bins, :], width_y - 1 - x, 1), pltpu.roll(slab, width_y - 1, 1))
        row = lambda k: faces[k, x:x + 1, :]
        return (
            slab * row(0)
            + row(low_x) * field[x, :bins, :]
            + row(high_x) * field[x + 2, :bins, :]
            + row(low_y) * before
            + row(high_y) * after
        )

    for x in range(width_x):
        moved[x] = stencil(state, y_recv, x, 1, 4, 5, 8)
        lam[x + 1, :bins, :] = wide_adj[pl.ds(x, bins, stride=width_x), :]

    def coagulate(first, second):
        current = jnp.concatenate([moved[first], moved[second]], axis=1)
        start = jnp.concatenate([lam[first + 1, :bins, :], lam[second + 1, :bins, :]], axis=1)
        saved = []
        for step in range(SUBSTEPS):
            spectra = dot(t_fwd[...], stacked(current))
            loss = spectra[4 * bins:]
            saved.append((current, spectra, loss))
            if step < SUBSTEPS - 1:
                both = product(spectra[:2 * bins], spectra[2 * bins:4 * bins])
                current = current + dot(t_gain[...], stacked(both)) - current * loss
        adjoint = start
        for step in reversed(range(SUBSTEPS)):
            current, spectra, loss = saved[step]
            spectra_l = dot(t_lam[...], stacked(adjoint))
            with_b = product_conj(spectra_l, spectra[2 * bins:4 * bins])
            with_a = product_conj(spectra_l, spectra[:2 * bins])
            terms = jnp.concatenate([stacked(with_b), stacked(with_a), stacked(adjoint * current)], axis=0)
            adjoint = adjoint + dot(t_lag[...], terms) - adjoint * loss
        on = jnp.concatenate([active[pl.ds(first, 1), :], active[pl.ds(second, 1), :]], axis=1) == 1
        result = jnp.where(on, adjoint, start)
        lam[first + 1, :bins, :] = result[:, :width_y]
        lam[second + 1, :bins, :] = result[:, width_y:]

    coagulate(0, width_x - 1)
    lam[1, bins:, :] = jnp.zeros((8, width_y), F32)
    lam[width_x, bins:, :] = jnp.zeros((8, width_y), F32)
    second_x = x_copies(lam, 4)
    for copy in second_x:
        copy.start()

    @pl.loop(0, width_x // 2 - 1)
    def _(block):
        coagulate(2 * block + 1, 2 * block + 2)

    edges(lam, z_send)
    second_y = y_copies(z_send, z_recv, 6)
    start_y(second_y, z_recv)
    for copy in second_x:
        copy.wait()
    wait_y(second_y)
    for x in range(width_x):
        out[pl.ds(x, bins, stride=width_x), :] = stencil(lam, z_recv, x, 2, 3, 6, 7)


def body(n_gx, n_gy, concentration, adjoint_next, sign_x, sign_y, courant_x, courant_y, active, kernel_a, kernel_b):
    bins, width_x, width_y = concentration.shape
    rows = bins * width_x
    tables = dft_tables(bins)
    vmem = pl.BlockSpec(memory_space=pltpu.VMEM)
    result = pl.pallas_call(
        functools.partial(kernel, n_gx, n_gy, width_x),
        out_shape=jax.ShapeDtypeStruct((rows, width_y), F32),
        in_specs=[vmem] * 12,
        out_specs=vmem,
        scratch_shapes=[
            pltpu.VMEM((rows, width_y), F32),
            pltpu.VMEM((rows, width_y), F32),
            pltpu.VMEM((width_x + 2, bins + 8, width_y), F32),
            pltpu.VMEM((width_x + 2, bins + 8, width_y), F32),
            pltpu.VMEM((2, bins + 2 * width_x, width_y), F32),
            pltpu.VMEM((2, bins + 2 * width_x, width_y), F32),
            pltpu.VMEM((2, bins, width_y), F32),
            pltpu.VMEM((2, bins, width_y), F32),
            pltpu.VMEM((width_x, bins, width_y), F32),
            pltpu.VMEM((9, width_x, width_y), F32),
            pltpu.VMEM((5 * bins, 3 * bins), BF16),
            pltpu.VMEM((bins, 6 * bins), BF16),
            pltpu.VMEM((2 * bins, 3 * bins), BF16),
            pltpu.VMEM((bins, 15 * bins), BF16),
            pltpu.SemaphoreType.DMA((8,)),
            pltpu.SemaphoreType.DMA((8,)),
        ],
        compiler_params=pltpu.CompilerParams(
            collective_id=0, has_side_effects=True, vmem_limit_bytes=48 * 1024 * 1024
        ),
    )(
        concentration.reshape(rows, width_y),
        adjoint_next.reshape(rows, width_y),
        sign_x, sign_y, courant_x, courant_y, active,
        kernel_a.reshape(1, bins), kernel_b.reshape(1, bins),
        *(jnp.asarray(t) for t in tables),
    )
    return result.reshape(bins, width_x, width_y)


def solution(mesh):
    return jax.shard_map(
        functools.partial(body, mesh.shape["gx"], mesh.shape["gy"]),
        mesh=mesh,
        in_specs=(
            P(None, "gx", "gy"),
            P(None, "gx", "gy"),
            P("gx", "gy"),
            P("gx", "gy"),
            P("gx", "gy"),
            P("gx", "gy"),
            P("gx", "gy"),
            P(),
            P(),
        ),
        out_specs=P(None, "gx", "gy"),
        check_vma=False,
    )
```

profile of v0, /device:TPU:0, one launch (start us, length us, event | category | flops | bytes accessed | tf_op | source)
XLA Modules:
  0.0 63.7 jit_solution(16728639025109251431)
XLA Ops:
  0.0 0.0 copy-start.10
  0.0 0.0 copy-start.11
  0.0 0.7 %copy-done.10 = f32[128]{0:T(128)S(1)} copy-done((f32[128]{0:T(128)S(1)}, f32[128]{0:T(128)}, u32[]{:S(2)}) %copy-start.10) | copy-done | bytes 536
  0.7 0.0 copy-done.11
  0.7 0.0 copy-start
  0.7 1.0 %copy-done = bf16[128,16,128]{2,1,0:T(8,128)(2,1)S(1)} copy-done((bf16[128,16,128]{2,1,0:T(8,128)(2,1)S(1)}, bf16[128,16,128]{2,1,0:T(8,128)(2,1)}, u32[]{:S(2)}) %copy-start) | copy-done | bytes 524312
  1.7 0.0 copy-start.1
  1.7 1.0 %copy-done.1 = bf16[128,16,128]{2,1,0:T(8,128)(2,1)S(1)} copy-done((bf16[128,16,128]{2,1,0:T(8,128)(2,1)S(1)}, bf16[128,16,128]{2,1,0:T(8,128)(2,1)}, u32[]{:S(2)}) %copy-start.1) | copy-done | bytes 524312
  2.8 0.0 copy-start.2
  2.8 0.9 %copy-done.2 = f32[128,256]{1,0:T(8,128)S(1)} copy-done((f32[128,256]{1,0:T(8,128)S(1)}, f32[128,256]{1,0:T(8,128)}, u32[]{:S(2)}) %copy-start.2) | copy-done | bytes 131096
  3.7 0.0 copy-start.3
  3.7 0.9 %copy-done.3 = f32[128,256]{1,0:T(8,128)S(1)} copy-done((f32[128,256]{1,0:T(8,128)S(1)}, f32[128,256]{1,0:T(8,128)}, u32[]{:S(2)}) %copy-start.3) | copy-done | bytes 131096
  4.6 0.0 copy-start.4
  4.6 0.9 %copy-done.4 = f32[256,128]{1,0:T(8,128)S(1)} copy-done((f32[256,128]{1,0:T(8,128)S(1)}, f32[256,128]{1,0:T(8,128)}, u32[]{:S(2)}) %copy-start.4) | copy-done | bytes 131096
  5.5 0.0 copy-start.5
  5.5 0.7 %copy-done.5 = s32[16,128]{1,0:T(8,128)S(1)} copy-done((s32[16,128]{1,0:T(8,128)S(1)}, s32[16,128]{1,0:T(8,128)}, u32[]{:S(2)}) %copy-start.5) | copy-done | bytes 8216
  6.2 0.0 copy-start.6
  6.2 0.7 %copy-done.6 = s32[16,128]{1,0:T(8,128)S(1)} copy-done((s32[16,128]{1,0:T(8,128)S(1)}, s32[16,128]{1,0:T(8,128)}, u32[]{:S(2)}) %copy-start.6) | copy-done | bytes 8216
  6.9 0.0 copy-start.7
  6.9 0.7 %copy-done.7 = f32[16,128]{1,0:T(8,128)S(1)} copy-done((f32[16,128]{1,0:T(8,128)S(1)}, f32[16,128]{1,0:T(8,128)}, u32[]{:S(2)}) %copy-start.7) | copy-done | bytes 8216
  7.6 0.7 %copy-done.8 = f32[16,128]{1,0:T(8,128)S(1)} copy-done((f32[16,128]{1,0:T(8,128)S(1)}, f32[16,128]{1,0:T(8,128)}, u32[]{:S(2)}) %copy-start.8) | copy-done | bytes 8216
  8.3 0.7 %copy-done.9 = s32[16,128]{1,0:T(8,128)S(1)} copy-done((s32[16,128]{1,0:T(8,128)S(1)}, s32[16,128]{1,0:T(8,128)}, u32[]{:S(2)}) %copy-start.9) | copy-done | bytes 8216
  9.0 53.7 %shard_map.118 = f32[2048,128]{1,0:T(8,128)S(1)} custom-call(bf16[2048,128]{1,0:T(8,128)(2,1)S(1)} %bitcast.6, bf16[2048,128]{1,0:T(8,128)(2,1)S(1)} %bitcast.7, s32[16,128]{1,0:T(8,128)S(1)} %copy-done.5, s32[16,128]{1,0:T(8,128)S(1)} %copy-done.6, f32[16,128]{1,0:T(8,128)S(1)} %copy-done.7, f32[16,128]{1,0:T(8,128)S(1)} %copy-done.8, ...), custom_call_target="tpu_custom_call" | custom-call | tf_op jit(solution)/shard_map/pallas_call | solution.py:292
  62.7 1.0 %copy.14 = f32[128,16,128]{2,1,0:T(8,128)} copy(f32[128,16,128]{2,1,0:T(8,128)S(1)} %bitcast.5) | data formatting | bytes 2097152
  (2 shorter events, 0.0 us)
Async XLA Ops:
  0.0 0.7 %copy-start.10 = (f32[128]{0:T(128)S(1)}, f32[128]{0:T(128)}, u32[]{:S(2)}) copy-start(f32[128]{0:T(128)} %param.19) | copy-start | bytes 1540
  0.0 0.7 %copy-start.11 = (f32[128]{0:T(128)S(1)}, f32[128]{0:T(128)}, u32[]{:S(2)}) copy-start(f32[128]{0:T(128)} %param.20) | copy-start | bytes 1540
  0.7 1.0 %copy-start = (bf16[128,16,128]{2,1,0:T(8,128)(2,1)S(1)}, bf16[128,16,128]{2,1,0:T(8,128)(2,1)}, u32[]{:S(2)}) copy-start(bf16[128,16,128]{2,1,0:T(8,128)(2,1)} %param.12) | copy-start | bytes 1572868
  1.7 1.0 %copy-start.1 = (bf16[128,16,128]{2,1,0:T(8,128)(2,1)S(1)}, bf16[128,16,128]{2,1,0:T(8,128)(2,1)}, u32[]{:S(2)}) copy-start(bf16[128,16,128]{2,1,0:T(8,128)(2,1)} %param.13) | copy-start | bytes 1572868
  2.8 0.9 %copy-start.2 = (f32[128,256]{1,0:T(8,128)S(1)}, f32[128,256]{1,0:T(8,128)}, u32[]{:S(2)}) copy-start(f32[128,256]{1,0:T(8,128)} %constant.8.clone.lag_ref) | copy-start | bytes 393220
  3.7 0.9 %copy-start.3 = (f32[128,256]{1,0:T(8,128)S(1)}, f32[128,256]{1,0:T(8,128)}, u32[]{:S(2)}) copy-start(f32[128,256]{1,0:T(8,128)} %constant.7.clone.gain_ref) | copy-start | bytes 393220
  4.6 0.9 %copy-start.4 = (f32[256,128]{1,0:T(8,128)S(1)}, f32[256,128]{1,0:T(8,128)}, u32[]{:S(2)}) copy-start(f32[256,128]{1,0:T(8,128)} %constant.6.clone.fwd_ref) | copy-start | bytes 393220
  5.5 0.7 %copy-start.5 = (s32[16,128]{1,0:T(8,128)S(1)}, s32[16,128]{1,0:T(8,128)}, u32[]{:S(2)}) copy-start(s32[16,128]{1,0:T(8,128)} %sx.1) | copy-start | bytes 24580
  6.2 0.7 %copy-start.6 = (s32[16,128]{1,0:T(8,128)S(1)}, s32[16,128]{1,0:T(8,128)}, u32[]{:S(2)}) copy-start(s32[16,128]{1,0:T(8,128)} %sy.1) | copy-start | bytes 24580
  6.9 0.7 %copy-start.7 = (f32[16,128]{1,0:T(8,128)S(1)}, f32[16,128]{1,0:T(8,128)}, u32[]{:S(2)}) copy-start(f32[16,128]{1,0:T(8,128)} %cx.1) | copy-start | bytes 24580
  7.6 0.7 %copy-start.8 = (f32[16,128]{1,0:T(8,128)S(1)}, f32[16,128]{1,0:T(8,128)}, u32[]{:S(2)}) copy-start(f32[16,128]{1,0:T(8,128)} %cy.1) | copy-start | bytes 24580
  8.3 0.7 %copy-start.9 = (s32[16,128]{1,0:T(8,128)S(1)}, s32[16,128]{1,0:T(8,128)}, u32[]{:S(2)}) copy-start(s32[16,128]{1,0:T(8,128)} %active.1) | copy-start | bytes 24580
where the time goes:
time: 64.1 us; the launch traced here: 63.7 us
  Pallas kernels  53.7 us (84%)
  local copies, waits for them, and re-layouts  9.92 us (15%)
    pallas_call x1, Pallas kernels, body(): pl.pallas_call(functools.partial(kernel, n_gx, n_gy, width_x), out_shape=...  53.7 us
    unnamed x25, local copies, waits for them, and re-layouts  9.92 us

commit v1 on v0

--- a/solution.py
+++ b/solution.py
@@ -62,11 +62,17 @@
 
 def kernel(
     n_gx, n_gy, width_x,
-    conc, adj, sx, sy, cx, cy, active, ka_ref, kb_ref, fwd_ref, gain_ref, lag_ref,
-    out,
-    wide, wide_adj, state, lam, y_send, y_recv, z_send, z_recv, moved, faces, t_fwd, t_gain, t_lam, t_lag,
-    send_sem, recv_sem,
+    *refs,
 ):
+    inputs, refs = refs[:12], refs[12:]
+    out, refs = refs[0], refs[1:]
+    fetched, refs = refs[:12], refs[12:]
+    conc, adj, sx, sy, cx, cy, active, ka_ref, kb_ref, fwd_ref, gain_ref, lag_ref = fetched
+    (wide, wide_adj, state, lam, y_send, y_recv, z_send, z_recv, moved, faces, t_fwd, t_gain, t_lam, t_lag,
+     send_sem, recv_sem, in_sem, out_sem) = refs
+    fetches = [pltpu.make_async_copy(i, f, in_sem.at[k]) for k, (i, f) in enumerate(zip(inputs, fetched))]
+    for k in (0, 2, 3, 4, 5, 1, 7, 8, 9, 10, 11, 6):
+        fetches[k].start()
     bins = ka_ref.shape[1]
     width_y = sx.shape[1]
     gx = lax.axis_index("gx")
@@ -91,6 +97,8 @@
     lane = lax.broadcasted_iota(jnp.int32, (bins, width_y), 1)
     lane_x = lax.broadcasted_iota(jnp.int32, (width_x, width_y), 1)
 
+    for k in (2, 3, 4, 5):
+        fetches[k].wait()
     plus_x = sx[...].astype(F32)
     plus_y = sy[...].astype(F32)
     inside = (lane_x + gy * width_y > 0).astype(F32)
@@ -99,6 +107,7 @@
     uy = cy[...] * plus_y * inside
     by = cy[...] * (1.0 - plus_y) * inside
 
+    fetches[0].wait()
     wide[...] = conc[...].astype(F32)
     for x in range(width_x):
         state[x + 1, :bins, :] = wide[pl.ds(x, bins, stride=width_x), :]
@@ -107,18 +116,16 @@
     state[1, bins + 2:, :] = jnp.zeros((6, width_y), F32)
     state[width_x, bins:, :] = jnp.zeros((8, width_y), F32)
 
-    def edges(field, buffer):
+    def edges(field, places):
         to_prv = jnp.zeros((bins, width_y), F32)
         to_nxt = jnp.zeros((bins, width_y), F32)
-        for x in range(width_x):
+        for x in places:
             slab = field[x + 1, :bins, :]
-            at_low = pltpu.roll(slab, x, 1) if x else slab
-            to_prv = jnp.where(lane == x, at_low, to_prv)
+            to_prv = jnp.where(lane == x, pltpu.roll(slab, x, 1), to_prv)
             to_nxt = jnp.where(lane == x, pltpu.roll(slab, x + 1, 1), to_nxt)
-        buffer[0, :bins, :] = to_prv
-        buffer[1, :bins, :] = to_nxt
-
-    edges(state, y_send)
+        return to_prv, to_nxt
+
+    y_send[0, :bins, :], y_send[1, :bins, :] = edges(state, range(width_x))
     y_send[0, bins:bins + width_x, :] = uy
     y_send[0, bins + width_x:, :] = by
     y_send[1, bins:, :] = jnp.zeros((2 * width_x, width_y), F32)
@@ -186,6 +193,8 @@
     for copy in first_x:
         copy.start()
 
+    for k in (7, 8, 9, 10, 11):
+        fetches[k].wait()
     ka_row, kb_row = ka_ref[...], kb_ref[...]
     ka_full = jnp.broadcast_to(ka_row, (bins, bins))
     kb_full = jnp.broadcast_to(kb_row, (bins, bins))
@@ -204,6 +213,8 @@
     t_lag[:, 6 * bins:12 * bins] = table3(kb_col2 * lag)
     t_lag[:, 12 * bins:] = table3(-pair)
 
+    fetches[1].wait()
+    fetches[6].wait()
     wide_adj[...] = adj[...].astype(F32)
 
     wait_y(first_y)
@@ -239,9 +250,20 @@
         moved[x] = stencil(state, y_recv, x, 1, 4, 5, 8)
         lam[x + 1, :bins, :] = wide_adj[pl.ds(x, bins, stride=width_x), :]
 
-    def coagulate(first, second):
-        current = jnp.concatenate([moved[first], moved[second]], axis=1)
-        start = jnp.concatenate([lam[first + 1, :bins, :], lam[second + 1, :bins, :]], axis=1)
+    lam[1, bins:, :] = jnp.zeros((8, width_y), F32)
+    lam[width_x, bins:, :] = jnp.zeros((8, width_y), F32)
+    half, quarter = width_x // 2, width_x // 4
+    second_x = x_copies(lam, 4)
+
+    def second_y(group):
+        return y_copies(z_send.at[group], z_recv.at[group], 6 + 2 * group)
+
+    @pl.loop(0, 2)
+    def _(group):
+        places = [p + quarter * group for p in range(quarter)]
+        places += [p + half - quarter * group for p in range(quarter, half)]
+        current = jnp.concatenate([moved[x] for x in places], axis=1)
+        start = jnp.concatenate([lam[x + 1, :bins, :] for x in places], axis=1)
         saved = []
         for step in range(SUBSTEPS):
             spectra = dot(t_fwd[...], stacked(current))
@@ -258,71 +280,74 @@
             with_a = product_conj(spectra_l, spectra[:2 * bins])
             terms = jnp.concatenate([stacked(with_b), stacked(with_a), stacked(adjoint * current)], axis=0)
             adjoint = adjoint + dot(t_lag[...], terms) - adjoint * loss
-        on = jnp.concatenate([active[pl.ds(first, 1), :], active[pl.ds(second, 1), :]], axis=1) == 1
+        on = jnp.concatenate([active[pl.ds(x, 1), :] for x in places], axis=1) == 1
         result = jnp.where(on, adjoint, start)
-        lam[first + 1, :bins, :] = result[:, :width_y]
-        lam[second + 1, :bins, :] = result[:, width_y:]
-
-    coagulate(0, width_x - 1)
-    lam[1, bins:, :] = jnp.zeros((8, width_y), F32)
-    lam[width_x, bins:, :] = jnp.zeros((8, width_y), F32)
-    second_x = x_copies(lam, 4)
-    for copy in second_x:
-        copy.start()
-
-    @pl.loop(0, width_x // 2 - 1)
-    def _(block):
-        coagulate(2 * block + 1, 2 * block + 2)
-
-    edges(lam, z_send)
-    second_y = y_copies(z_send, z_recv, 6)
-    start_y(second_y, z_recv)
+        for index, x in enumerate(places):
+            lam[x + 1, :bins, :] = result[:, index * width_y:(index + 1) * width_y]
+
+        @pl.when(group == 0)
+        def _():
+            for copy in second_x:
+                copy.start()
+
+        z_send[group, 0], z_send[group, 1] = edges(lam, places)
+        start_y(second_y(group), z_recv.at[group])
+
+    outer = [*range(quarter), *range(half + quarter, width_x)]
     for copy in second_x:
         copy.wait()
-    wait_y(second_y)
-    for x in range(width_x):
-        out[pl.ds(x, bins, stride=width_x), :] = stencil(lam, z_recv, x, 2, 3, 6, 7)
+    writes = []
+    for group, places in enumerate((outer, range(quarter, half + quarter))):
+        wait_y(second_y(group))
+        for x in places:
+            moved[x] = stencil(lam, z_recv.at[group], x, 2, 3, 6, 7)
+            writes.append(pltpu.make_async_copy(moved.at[x], out.at[:, x, :], out_sem.at[x]))
+            writes[-1].start()
+    for copy in writes:
+        copy.wait()
 
 
 def body(n_gx, n_gy, concentration, adjoint_next, sign_x, sign_y, courant_x, courant_y, active, kernel_a, kernel_b):
     bins, width_x, width_y = concentration.shape
     rows = bins * width_x
     tables = dft_tables(bins)
-    vmem = pl.BlockSpec(memory_space=pltpu.VMEM)
-    result = pl.pallas_call(
+    operands = (
+        concentration.reshape(rows, width_y),
+        adjoint_next.reshape(rows, width_y),
+        sign_x, sign_y, courant_x, courant_y, active,
+        kernel_a.reshape(1, bins), kernel_b.reshape(1, bins),
+        *(jnp.asarray(t) for t in tables),
+    )
+    return pl.pallas_call(
         functools.partial(kernel, n_gx, n_gy, width_x),
-        out_shape=jax.ShapeDtypeStruct((rows, width_y), F32),
-        in_specs=[vmem] * 12,
-        out_specs=vmem,
+        out_shape=jax.ShapeDtypeStruct((bins, width_x, width_y), F32),
+        in_specs=[pl.BlockSpec(memory_space=pltpu.HBM)] * 12,
+        out_specs=pl.BlockSpec(memory_space=pltpu.HBM),
         scratch_shapes=[
+            *(pltpu.VMEM(a.shape, a.dtype) for a in operands),
             pltpu.VMEM((rows, width_y), F32),
             pltpu.VMEM((rows, width_y), F32),
             pltpu.VMEM((width_x + 2, bins + 8, width_y), F32),
             pltpu.VMEM((width_x + 2, bins + 8, width_y), F32),
             pltpu.VMEM((2, bins + 2 * width_x, width_y), F32),
             pltpu.VMEM((2, bins + 2 * width_x, width_y), F32),
-            pltpu.VMEM((2, bins, width_y), F32),
-            pltpu.VMEM((2, bins, width_y), F32),
+            pltpu.VMEM((2, 2, bins, width_y), F32),
+            pltpu.VMEM((2, 2, bins, width_y), F32),
             pltpu.VMEM((width_x, bins, width_y), F32),
             pltpu.VMEM((9, width_x, width_y), F32),
             pltpu.VMEM((5 * bins, 3 * bins), BF16),
             pltpu.VMEM((bins, 6 * bins), BF16),
             pltpu.VMEM((2 * bins, 3 * bins), BF16),
             pltpu.VMEM((bins, 15 * bins), BF16),
-            pltpu.SemaphoreType.DMA((8,)),
-            pltpu.SemaphoreType.DMA((8,)),
+            pltpu.SemaphoreType.DMA((10,)),
+            pltpu.SemaphoreType.DMA((10,)),
+            pltpu.SemaphoreType.DMA((12,)),
+            pltpu.SemaphoreType.DMA((width_x,)),
         ],
         compiler_params=pltpu.CompilerParams(
-            collective_id=0, has_side_effects=True, vmem_limit_bytes=48 * 1024 * 1024
+            collective_id=0, has_side_effects=True, vmem_limit_bytes=60 * 1024 * 1024
         ),
-    )(
-        concentration.reshape(rows, width_y),
-        adjoint_next.reshape(rows, width_y),
-        sign_x, sign_y, courant_x, courant_y, active,
-        kernel_a.reshape(1, bins), kernel_b.reshape(1, bins),
-        *(jnp.asarray(t) for t in tables),
-    )
-    return result.reshape(bins, width_x, width_y)
+    )(*operands)
 
 
 def solution(mesh):

time: 64.1 us -> 35.1 us (0.55)
  Pallas kernels: 53.7 us -> 32.6 us
  local copies, waits for them, and re-layouts: 9.92 us -> 2.26 us
    pallas_call x1, Pallas kernels: 53.7 us -> 32.6 us  [body(): pl.pallas_call(functools.partial(kernel, n_gx, n_gy, width_x), out_shape=...]
    unnamed x25 -> x1, local copies, waits for them, and re-layouts: 9.92 us -> 2.26 us
where the time goes in v1:
time: 35.1 us; the launch traced here: 34.9 us
  Pallas kernels  32.6 us (93%)
  local copies, waits for them, and re-layouts  2.26 us (6%)
    pallas_call x1, Pallas kernels, body(): pl.pallas_call(functools.partial(kernel, n_gx, n_gy, width_x), out_shape=...  32.6 us
    unnamed x1, local copies, waits for them, and re-layouts  2.26 us

profile of v1, /device:TPU:0, one launch (start us, length us, event | category | flops | bytes accessed | tf_op | source)
XLA Modules:
  0.0 34.9 jit_solution(11106740897460697403)
XLA Ops:
  0.0 32.6 %shard_map.118 = f32[128,16,128]{2,1,0:T(8,128)} custom-call(bf16[2048,128]{1,0:T(8,128)(2,1)} %bitcast.4, bf16[2048,128]{1,0:T(8,128)(2,1)} %bitcast.5, s32[16,128]{1,0:T(8,128)} %refs_2_.1, s32[16,128]{1,0:T(8,128)} %refs_3_.1, f32[16,128]{1,0:T(8,128)} %refs_4_.1, f32[16,128]{1,0:T(8,128)} %refs_5_.1, s32[16,128]{1,0:T(8,128)} %refs_6_.1, ...), custom_call_target="tpu_custom_call" | custom-call | tf_op jit(solution)/shard_map/pallas_call | solution.py:321
  32.6 2.3 %copy.14 = f32[128,16,128]{2,1,0:T(8,128)} copy(f32[128,16,128]{2,1,0:T(8,128)} %shard_map.118) | data formatting | bytes 2097152

commit v2 on v1

--- a/solution.py
+++ b/solution.py
@@ -69,7 +69,7 @@
     fetched, refs = refs[:12], refs[12:]
     conc, adj, sx, sy, cx, cy, active, ka_ref, kb_ref, fwd_ref, gain_ref, lag_ref = fetched
     (wide, wide_adj, state, lam, y_send, y_recv, z_send, z_recv, moved, faces, t_fwd, t_gain, t_lam, t_lag,
-     send_sem, recv_sem, in_sem, out_sem) = refs
+     send_sem, recv_sem, in_sem) = refs
     fetches = [pltpu.make_async_copy(i, f, in_sem.at[k]) for k, (i, f) in enumerate(zip(inputs, fetched))]
     for k in (0, 2, 3, 4, 5, 1, 7, 8, 9, 10, 11, 6):
         fetches[k].start()
@@ -109,26 +109,12 @@
 
     fetches[0].wait()
     wide[...] = conc[...].astype(F32)
-    for x in range(width_x):
+    for x in (0, width_x - 1):
         state[x + 1, :bins, :] = wide[pl.ds(x, bins, stride=width_x), :]
     state[1, bins:bins + 1, :] = ux[0:1]
     state[1, bins + 1:bins + 2, :] = bx[0:1]
     state[1, bins + 2:, :] = jnp.zeros((6, width_y), F32)
     state[width_x, bins:, :] = jnp.zeros((8, width_y), F32)
-
-    def edges(field, places):
-        to_prv = jnp.zeros((bins, width_y), F32)
-        to_nxt = jnp.zeros((bins, width_y), F32)
-        for x in places:
-            slab = field[x + 1, :bins, :]
-            to_prv = jnp.where(lane == x, pltpu.roll(slab, x, 1), to_prv)
-            to_nxt = jnp.where(lane == x, pltpu.roll(slab, x + 1, 1), to_nxt)
-        return to_prv, to_nxt
-
-    y_send[0, :bins, :], y_send[1, :bins, :] = edges(state, range(width_x))
-    y_send[0, bins:bins + width_x, :] = uy
-    y_send[0, bins + width_x:, :] = by
-    y_send[1, bins:, :] = jnp.zeros((2 * width_x, width_y), F32)
 
     def x_copies(field, base):
         return (
@@ -142,6 +128,27 @@
                 device_id=(nxt_x, gy), device_id_type=mesh_id),
         )
 
+    pl.semaphore_wait(barrier, 2 + has_prv.astype(jnp.int32) + has_nxt.astype(jnp.int32))
+    first_x = x_copies(state, 0)
+    for copy in first_x:
+        copy.start()
+    for x in range(1, width_x - 1):
+        state[x + 1, :bins, :] = wide[pl.ds(x, bins, stride=width_x), :]
+
+    def edges(field, places):
+        to_prv = jnp.zeros((bins, width_y), F32)
+        to_nxt = jnp.zeros((bins, width_y), F32)
+        for x in places:
+            slab = field[x + 1, :bins, :]
+            to_prv = jnp.where(lane == x, pltpu.roll(slab, x, 1), to_prv)
+            to_nxt = jnp.where(lane == x, pltpu.roll(slab, x + 1, 1), to_nxt)
+        return to_prv, to_nxt
+
+    y_send[0, :bins, :], y_send[1, :bins, :] = edges(state, range(width_x))
+    y_send[0, bins:bins + width_x, :] = uy
+    y_send[0, bins + width_x:, :] = by
+    y_send[1, bins:, :] = jnp.zeros((2 * width_x, width_y), F32)
+
     def y_copies(source, target, base):
         return (
             pltpu.make_async_remote_copy(
@@ -186,12 +193,8 @@
             to_nxt.wait_send()
             to_prv.wait_recv()
 
-    pl.semaphore_wait(barrier, 2 + has_prv.astype(jnp.int32) + has_nxt.astype(jnp.int32))
-    first_x = x_copies(state, 0)
     first_y = y_copies(y_send, y_recv, 2)
     start_y(first_y, y_recv)
-    for copy in first_x:
-        copy.start()
 
     for k in (7, 8, 9, 10, 11):
         fetches[k].wait()
@@ -296,15 +299,10 @@
     outer = [*range(quarter), *range(half + quarter, width_x)]
     for copy in second_x:
         copy.wait()
-    writes = []
     for group, places in enumerate((outer, range(quarter, half + quarter))):
         wait_y(second_y(group))
         for x in places:
-            moved[x] = stencil(lam, z_recv.at[group], x, 2, 3, 6, 7)
-            writes.append(pltpu.make_async_copy(moved.at[x], out.at[:, x, :], out_sem.at[x]))
-            writes[-1].start()
-    for copy in writes:
-        copy.wait()
+            out[pl.ds(x, bins, stride=width_x), :] = stencil(lam, z_recv.at[group], x, 2, 3, 6, 7)
 
 
 def body(n_gx, n_gy, concentration, adjoint_next, sign_x, sign_y, courant_x, courant_y, active, kernel_a, kernel_b):
@@ -318,11 +316,11 @@
         kernel_a.reshape(1, bins), kernel_b.reshape(1, bins),
         *(jnp.asarray(t) for t in tables),
     )
-    return pl.pallas_call(
+    result = pl.pallas_call(
         functools.partial(kernel, n_gx, n_gy, width_x),
-        out_shape=jax.ShapeDtypeStruct((bins, width_x, width_y), F32),
+        out_shape=pltpu.VMEM((rows, width_y), F32),
         in_specs=[pl.BlockSpec(memory_space=pltpu.HBM)] * 12,
-        out_specs=pl.BlockSpec(memory_space=pltpu.HBM),
+        out_specs=pl.BlockSpec(memory_space=pltpu.VMEM),
         scratch_shapes=[
             *(pltpu.VMEM(a.shape, a.dtype) for a in operands),
             pltpu.VMEM((rows, width_y), F32),
@@ -342,12 +340,12 @@
             pltpu.SemaphoreType.DMA((10,)),
             pltpu.SemaphoreType.DMA((10,)),
             pltpu.SemaphoreType.DMA((12,)),
-            pltpu.SemaphoreType.DMA((width_x,)),
         ],
         compiler_params=pltpu.CompilerParams(
             collective_id=0, has_side_effects=True, vmem_limit_bytes=60 * 1024 * 1024
         ),
     )(*operands)
+    return result.reshape(bins, width_x, width_y)
 
 
 def solution(mesh):

time: 35.1 us -> 33.7 us (0.960)
  local copies, waits for them, and re-layouts: 2.26 us -> 0.97 us
    unnamed x1, local copies, waits for them, and re-layouts: 2.26 us -> 0.97 us
where the time goes in v2:
time: 33.7 us; the launch traced here: 33.5 us
  Pallas kernels  32.6 us (97%)
  local copies, waits for them, and re-layouts  0.97 us (3%)
    pallas_call x1, Pallas kernels, body(): pl.pallas_call(functools.partial(kernel, n_gx, n_gy, width_x), out_shape=...  32.6 us
    unnamed x1, local copies, waits for them, and re-layouts  0.97 us

profile of v2, /device:TPU:0, one launch (start us, length us, event | category | flops | bytes accessed | tf_op | source)
XLA Modules:
  0.0 33.5 jit_solution(3575182676676336269)
XLA Ops:
  0.0 32.6 %shard_map.118 = f32[2048,128]{1,0:T(8,128)S(1)} custom-call(bf16[2048,128]{1,0:T(8,128)(2,1)} %bitcast.6, bf16[2048,128]{1,0:T(8,128)(2,1)} %bitcast.7, s32[16,128]{1,0:T(8,128)} %refs_2_.1, s32[16,128]{1,0:T(8,128)} %refs_3_.1, f32[16,128]{1,0:T(8,128)} %refs_4_.1, f32[16,128]{1,0:T(8,128)} %refs_5_.1, s32[16,128]{1,0:T(8,128)} %refs_6_.1, ...), custom_call_target="tpu_custom_call" | custom-call | tf_op jit(solution)/shard_map/pallas_call | solution.py:319
  32.6 1.0 %copy.14 = f32[128,16,128]{2,1,0:T(8,128)} copy(f32[128,16,128]{2,1,0:T(8,128)S(1)} %bitcast.5) | data formatting | bytes 2097152

commit v3 on v2

--- a/solution.py
+++ b/solution.py
@@ -219,6 +219,8 @@
     fetches[1].wait()
     fetches[6].wait()
     wide_adj[...] = adj[...].astype(F32)
+    for x in range(width_x):
+        lam[x + 1, :bins, :] = wide_adj[pl.ds(x, bins, stride=width_x), :]
 
     wait_y(first_y)
     for copy in first_x:
@@ -251,7 +253,6 @@
 
     for x in range(width_x):
         moved[x] = stencil(state, y_recv, x, 1, 4, 5, 8)
-        lam[x + 1, :bins, :] = wide_adj[pl.ds(x, bins, stride=width_x), :]
 
     lam[1, bins:, :] = jnp.zeros((8, width_y), F32)
     lam[width_x, bins:, :] = jnp.zeros((8, width_y), F32)

time: 33.7 us -> 33.3 us (0.988)
  Pallas kernels: 32.6 us -> 32.2 us
    pallas_call x1, Pallas kernels: 32.6 us -> 32.2 us  [body(): pl.pallas_call(functools.partial(kernel, n_gx, n_gy, width_x), out_shape=...]
where the time goes in v3:
time: 33.3 us; the launch traced here: 33.2 us
  Pallas kernels  32.2 us (97%)
  local copies, waits for them, and re-layouts  0.97 us (3%)
    pallas_call x1, Pallas kernels, body(): pl.pallas_call(functools.partial(kernel, n_gx, n_gy, width_x), out_shape=...  32.2 us
    unnamed x1, local copies, waits for them, and re-layouts  0.97 us

profile of v3, /device:TPU:0, one launch (start us, length us, event | category | flops | bytes accessed | tf_op | source)
XLA Modules:
  0.0 33.2 jit_solution(7866193727101135835)
XLA Ops:
  0.0 32.2 %shard_map.118 = f32[2048,128]{1,0:T(8,128)S(1)} custom-call(bf16[2048,128]{1,0:T(8,128)(2,1)} %bitcast.6, bf16[2048,128]{1,0:T(8,128)(2,1)} %bitcast.7, s32[16,128]{1,0:T(8,128)} %refs_2_.1, s32[16,128]{1,0:T(8,128)} %refs_3_.1, f32[16,128]{1,0:T(8,128)} %refs_4_.1, f32[16,128]{1,0:T(8,128)} %refs_5_.1, s32[16,128]{1,0:T(8,128)} %refs_6_.1, ...), custom_call_target="tpu_custom_call" | custom-call | tf_op jit(solution)/shard_map/pallas_call | solution.py:320
  32.2 1.0 %copy.14 = f32[128,16,128]{2,1,0:T(8,128)} copy(f32[128,16,128]{2,1,0:T(8,128)S(1)} %bitcast.5) | data formatting | bytes 2097152
